TPU v7x, 512 devices: a whole 4x8x8 slice. The times are simulated.
512 devices in a mesh: dp: 64 (over x, y, z_lo), node: 8 (over z_hi, core).
Axes of the slice: x: 4, y: 8, z: 8 (z_hi: 4, z_lo: 2; z = z_hi * 2 + z_lo), core: 2. Of those that a mesh axis runs over, the one named last changes fastest.
Arguments:
- hidden: bfloat16 [131072, 2048], P(('dp', 'node')), may hold values from -24 to 24
- queries: bfloat16 [131072, 1024], P(('dp', 'node')), may hold values from -64 to 64
- cotangent: bfloat16 [131072, 1024], P(('dp', 'node')), may hold values from -6 to 6
- segments: int32 [512, 256], P(('dp', 'node')), may hold values from 0 to 3, never falling along the last dimension, each value on 1 to 128 neighbouring positions
- kv_weight: bfloat16 [2048, 512], P(('dp', 'node')), may hold values from -0.125 to 0.125
Outputs:
- grad_hidden: bfloat16 [131072, 2048], P(('dp', 'node'))
- grad_weights: float32 [2048, 512], P(('dp', 'node'))
Inputs may be any that keep to these rules, and one draw needn't show every extreme that they name: `segments`: within each row the segment numbers never fall.
All inputs are finite; a program needn't handle non-finite values.
Results may differ from a plain program's by a relative error of at most 0.013.
The roundings to bfloat16 on the way count: a program that leaves them out, or rounds other values in their place, can miss the bound.
Values may be sent and summed in bfloat16 or wider, within the bound.
A program may use at most 64 MiB of HBM per device.

v0:
```python
import math

import jax
import jax.numpy as jnp
from jax import lax
from jax.sharding import PartitionSpec as P

HEAD = 64
Q_HEADS = 16
KV_HEADS = 4


def attend_backward(queries, cotangent, seg_row, keys_flat, values_flat):
    tok = queries.shape[0]
    group = Q_HEADS // KV_HEADS
    keys = keys_flat.reshape(tok, KV_HEADS, HEAD)
    values = values_flat.reshape(tok, KV_HEADS, HEAD)
    query_heads = queries.reshape(tok, KV_HEADS, group, HEAD)
    cot_heads = cotangent.reshape(tok, KV_HEADS, group, HEAD)
    position = jnp.arange(tok, dtype=jnp.int32)
    allowed = (seg_row[:, None] == seg_row[None, :]) & (position[:, None] >= position[None, :])
    scores = (
        jnp.einsum("qhgd,khd->hgqk", query_heads, keys, preferred_element_type=jnp.float32) * 0.125
    )
    scores = jnp.where(allowed, scores, -1e30)
    top = jnp.max(scores, axis=-1, keepdims=True)
    expo = jnp.exp(scores - top)
    prob = expo / jnp.sum(expo, axis=-1, keepdims=True)
    prob_b = prob.astype(jnp.bfloat16)
    attended = jnp.einsum("hgqk,khd->qhgd", prob_b, values, preferred_element_type=jnp.float32)
    delta = jnp.sum(cot_heads.astype(jnp.float32) * attended, axis=-1)
    grad_values = jnp.einsum(
        "hgqk,qhgd->khd", prob_b, cot_heads, preferred_element_type=jnp.float32
    ).astype(jnp.bfloat16)
    grad_prob = jnp.einsum("qhgd,khd->hgqk", cot_heads, values, preferred_element_type=jnp.float32)
    grad_scores = (prob * (grad_prob - jnp.transpose(delta, (1, 2, 0))[..., None]) * 0.125).astype(
        jnp.bfloat16
    )
    grad_keys = jnp.einsum(
        "hgqk,qhgd->khd", grad_scores, query_heads, preferred_element_type=jnp.float32
    ).astype(jnp.bfloat16)
    return (grad_keys.reshape(tok, -1), grad_values.reshape(tok, -1))


def term_for(source, right):
    return lax.dot_general(
        source, right, (((0,), (0,)), ((), ())), preferred_element_type=jnp.float32
    )


def on_device(hidden, queries, cotangent, segments, kv_weight):
    full_weight = lax.all_gather(kv_weight, ("dp", "node"), axis=0, tiled=True)
    model_width = full_weight.shape[0]
    key_width = full_weight.shape[1] // 2
    kv = jnp.dot(hidden, full_weight, preferred_element_type=jnp.float32).astype(jnp.bfloat16)
    grad_keys, grad_values = attend_backward(
        queries, cotangent, segments[0], kv[:, :key_width], kv[:, key_width:]
    )
    grad_kv = jnp.concatenate([grad_keys, grad_values], axis=1)
    share = model_width // lax.axis_size("node")
    secondary = lax.dynamic_slice_in_dim(full_weight, lax.axis_index("node") * share, share, 0)
    grad_hidden = lax.dot_general(
        grad_kv,
        lax.all_gather(secondary, "node", axis=0, tiled=True),
        (((1,), (1,)), ((), ())),
        preferred_element_type=jnp.float32,
    ).astype(jnp.bfloat16)
    tok_rows = hidden.shape[0]
    scale = 1.0 / math.sqrt(lax.axis_size(("dp", "node")) * tok_rows)
    summed = lax.psum_scatter(
        term_for(hidden, grad_kv), ("dp", "node"), scatter_dimension=0, tiled=True
    )
    return (grad_hidden, summed * scale)


def solution(mesh):
    placed = (
        P(("dp", "node"), None),
        P(("dp", "node"), None),
        P(("dp", "node"), None),
        P(("dp", "node"), None),
        P(("dp", "node"), None),
    )
    return jax.shard_map(
        on_device,
        mesh=mesh,
        in_specs=placed,
        out_specs=(P(("dp", "node"), None), P(("dp", "node"), None)),
        check_vma=False,
    )
```

profile of v0, /device:TPU:1, one launch (start us, length us, event | category | flops | bytes accessed | tf_op | source)
XLA Modules:
  0.0 1124.7 jit_solution(4323679741189468007)
XLA Ops:
  7.2 0.0 all-gather.6.cloned.1.call-start
  7.2 0.7 all-gather.6.cloned.1.call-update
  7.9 0.0 all-reduce.3.cloned.1.call-start
  8.0 1.2 copy.22
  9.2 1.2 copy.24
  10.5 0.9 fusion.17
  11.3 763.4 %all-gather.6.cloned.1.call-done = bf16[512,4,512]{2,1,0:T(4,128)(2,1)} async-done(((bf16[1,4,512]{2,1,0:T(4,128)(2,1)}), bf16[512,4,512]{2,1,0:T(4,128)(2,1)}) %all-gather.6.cloned.1.call-update) | async-done | bytes 2097168 | tf_op jit(solution)/shard_map/all_gather | solution.py:52
  774.7 4.0 reshape.33
  778.7 2.3 convolution_convert_fusion.1
  781.0 0.1 copy.21
  781.1 0.1 copy.23
  781.2 3.4 fusion.24
  784.6 2.6 fusion.8
  787.2 0.8 fusion.13
  788.0 0.5 fusion.11
  788.5 3.6 fusion.14
  792.0 2.7 convolution_bitcast_fusion
  794.8 0.0 all-gather.4.cloned.1.call-start
  794.8 1.7 constant_dynamic-slice_fusion
  796.5 278.7 %all-reduce.3.cloned.1.call-done = f32[2048,512]{0,1:T(8,128)} async-done(((f32[2048,512]{0,1:T(8,128)}), f32[2048,512]{0,1:T(8,128)}) %all-reduce.3.cloned.1.call-update) | async-done | bytes 4194320
  1075.3 1.1 dynamic-slice_multiply_fusion
  1076.4 0.7 copy.28
  1077.1 37.8 %all-gather.4.cloned.1.call-done = bf16[2048,512]{1,0:T(8,128)(2,1)} async-done(((bf16[256,512]{1,0:T(8,128)(2,1)}), bf16[2048,512]{1,0:T(8,128)(2,1)}) %all-gather.4.cloned.1.call-update) | async-done | bytes 2097168 | tf_op jit(solution)/shard_map/all_gather | solution.py:64
  1114.8 3.3 convolution_convert_fusion
  (5 shorter events, 0.1 us)
Async XLA Ops:
  7.2 771.5 %copy-start = (bf16[256,2048]{1,0:T(8,128)(2,1)S(1)}, bf16[256,2048]{1,0:T(8,128)(2,1)}, u32[]{:S(2)}) copy-start(bf16[256,2048]{1,0:T(8,128)(2,1)} %param.5) | copy-start | bytes 3145732
  7.2 767.5 %all-gather.6.cloned.1.call-start = ((), (), s32[]{:S(2)}) async-start(), calls=%async_computation.1 | async-start | bytes 2101248 | tf_op jit(solution)/shard_map/all_gather | solution.py:52
  7.9 1067.4 %all-reduce.3.cloned.1.call-start = ((), (), s32[]{:S(2)}) async-start(), calls=%async_computation.2 | async-start | bytes 8388608
  794.8 320.1 %all-gather.4.cloned.1.call-start = ((), (), s32[]{:S(2)}) async-start(), calls=%async_computation | async-start | bytes 2359296 | tf_op jit(solution)/shard_map/all_gather | solution.py:64
Sparse Core Ops, SparseCore 0:
  10.1 764.5 all-gather.5
  794.9 280.3 all-reduce.2
  1078.0 36.7 all-gather.3
where the time goes:
time: 1130 us; the launch traced here: 1120 us
  waiting for transfers between devices  1080 us (96%)
  matrix products  16.5 us (1%)
  between operations  13.8 us (1%)
    all_gather x1, waiting for transfers between devices, on_device(): full_weight = lax.all_gather(kv_weight, ('dp', 'node'), axis=0, tiled=True)  763 us
    unnamed x4, waiting for transfers between devices  279 us
    all_gather x1, waiting for transfers between devices, on_device(): lax.all_gather(secondary, 'node', axis=0, tiled=True)  37.8 us
  transfers between devices with their start and end apart: 3, of which 3 were waited for; matrix products, arithmetic and copies ran while one was open for 1% of the time, Pallas kernels for 0%

commit v1 on v0

v1 whole, which is shorter than its diff:
```python
import functools
import math

import jax
import jax.numpy as jnp
from jax import lax
from jax.experimental import pallas as pl
from jax.experimental.pallas import tpu as pltpu
from jax.sharding import PartitionSpec as P

HEAD = 64
KV_HEADS = 4
GROUP = 4
TOK = 256
HALF = 128
NX, NY, NZL, NZH, NC = 4, 8, 2, 4, 2
NZC = 16
CH = KV_HEADS
MESH = pl.DeviceIdType.MESH
F32, BF16 = jnp.float32, jnp.bfloat16
NT = (((1,), (1,)), ((), ()))
NEAR = (1, 7, 2, 6, 3, 5, 4)


def dot(a, b):
    return jnp.dot(a, b, preferred_element_type=F32)


def natural(w_ref, j, x):
    both = jnp.stack([w_ref[j, 0, x], w_ref[j, 1, x]], axis=1)
    return both.reshape(512, 128)


def kernel(
    scale,
    hid_hbm, que_hbm, cot_hbm, seg_hbm, kvw_hbm,
    gh_hbm, gw_ref,
    hid, que, cot, seg, kvw,
    blk, zrecv, w, h_t, q_t, c_t, q_n, c_n, bias_a, bias_b,
    s_a, s_b, d_a, d_b, p_a, p_b, ds_a, ds_b, gkv,
    g_send, c_recv, x_send, x_recv, y_send, y_recv, z_sum, z_send, f_recv, gh,
    in_sem, out_sem,
    az_s, az_r, ay_s, ay_r, ax_s, ax_r, ac_s, ac_r,
    rc_s, rc_r, rx_s, rx_r, ry_s, ry_r, rz_s, rz_r,
):
    dp, node = lax.axis_index("dp"), lax.axis_index("node")
    x = dp // (NY * NZL)
    y = (dp // NZL) % NY
    zl = dp % NZL
    zh = node // NC
    core = node % NC
    z = zh * NZL + zl

    def at(x_, y_, z_, c_):
        return ((x_ * NY + y_) * NZL + z_ % NZL, (z_ // NZL) * NC + c_)

    ins = [
        pltpu.make_async_copy(kvw_hbm, kvw, in_sem.at[0]),
        pltpu.make_async_copy(hid_hbm, hid, in_sem.at[1]),
        pltpu.make_async_copy(que_hbm, que, in_sem.at[2]),
        pltpu.make_async_copy(cot_hbm, cot, in_sem.at[3]),
        pltpu.make_async_copy(seg_hbm, seg, in_sem.at[4]),
    ]
    for cp in ins:
        cp.start()

    barrier = pltpu.get_barrier_semaphore()

    def greet_z(k, carry):
        other = (z * NC + core + k) % NZC
        pl.semaphore_signal(
            barrier, inc=1, device_id=at(x, y, other // NC, other % NC), device_id_type=MESH
        )
        return carry

    def greet_y(k, carry):
        pl.semaphore_signal(
            barrier, inc=1, device_id=at(x, (y + k) % NY, z, core), device_id_type=MESH
        )
        return carry

    def greet_x(k, carry):
        pl.semaphore_signal(
            barrier, inc=1, device_id=at((x + k) % NX, y, z, core), device_id_type=MESH
        )
        return carry

    lax.fori_loop(1, NZC, greet_z, 0)
    lax.fori_loop(1, NY, greet_y, 0)
    lax.fori_loop(1, NX, greet_x, 0)

    ins[0].wait()
    own = kvw[...].astype(F32)
    blk[...] = jnp.concatenate(
        [
            jnp.concatenate([own[:, j * 64 : j * 64 + 64], own[:, 256 + j * 64 : 320 + j * 64]], axis=1)
            for j in range(CH)
        ],
        axis=0,
    ).astype(BF16)
    pl.semaphore_wait(barrier, (NZC - 1) + (NY - 1) + (NX - 1))

    slot = zh * NC + core

    def gather_z(a, b, remote):
        if not remote:
            return pltpu.make_async_copy(blk, zrecv.at[slot], az_r)
        return pltpu.make_async_remote_copy(
            blk, zrecv.at[slot], az_s, az_r,
            device_id=at(x, y, ((zh + a) % NZH) * NZL + (zl + b) % NZL, zl), device_id_type=MESH,
        )

    for a in range(NZH):
        for b in range(NZL):
            if a or b:
                gather_z(a, b, True).start()
    home = core == zl

    @pl.when(home)
    def _():
        gather_z(0, 0, False).start()

    @pl.when(jnp.logical_not(home))
    def _():
        gather_z(0, 0, True).start()

    ins[1].wait()
    for t in range(16):
        cols = hid[:, t * 128 : (t + 1) * 128].astype(F32)
        turned = jnp.transpose(cols).astype(BF16)
        for half in range(4):
            row = t * 2 + half // 2
            h_t[half % 2, row * 32 : row * 32 + 32, :] = turned[half * 32 : half * 32 + 32, :]

    pltpu.make_async_copy(zrecv, zrecv, az_r).wait()
    r_out = lax.broadcasted_iota(jnp.int32, (128, 128), 0)
    r_in = lax.broadcasted_iota(jnp.int32, (128, 128), 1)
    wanted = ((r_out // 4) % 8) * 16 + (r_out // 32) * 4 + r_out % 4
    mine = dot((r_in == wanted).astype(BF16), zrecv[...].reshape(128, 128)).astype(BF16)
    w[:, core, x, y] = mine.reshape(CH, 32, 128)

    def copy_y(j, k):
        return pltpu.make_async_remote_copy(
            w.at[j, core, x, y], w.at[j, core, x, y], ay_s, ay_r.at[j, k - 1],
            device_id=at(x, (y + k) % NY, z, core), device_id_type=MESH,
        )

    def wait_y(j, k):
        src = (y + NY - k) % NY
        pltpu.make_async_copy(
            w.at[j, core, x, src], w.at[j, core, x, src], ay_r.at[j, k - 1]
        ).wait()

    def copy_x(j, yb, a):
        return pltpu.make_async_remote_copy(
            w.at[j, core, x, yb], w.at[j, core, x, yb], ax_s, ax_r.at[j],
            device_id=at((x + a) % NX, y, z, core), device_id_type=MESH,
        )

    def send_y(j, carry):
        for k in NEAR:
            copy_y(j, k).start()
        for a in (2, 1, 3):
            copy_x(j, y, a).start()
        return carry

    lax.fori_loop(0, CH, send_y, 0)

    ins[2].wait()
    ins[3].wait()
    lane = lax.broadcasted_iota(jnp.int32, (TOK, 128), 1)
    low = lane < 64
    zeros = jnp.zeros((64, 512), BF16)
    for j in range(CH):
        for part in range(2):
            q_t[j, part, 64:128, :] = zeros
            c_t[j, part, 0:64, :] = zeros
        for pair in range(2):
            tile = j * 2 + pair
            q = que[:, tile * 128 : (tile + 1) * 128].astype(F32) * 0.125
            c = cot[:, tile * 128 : (tile + 1) * 128].astype(F32)
            q_turn, c_turn = jnp.transpose(q).astype(BF16), jnp.transpose(c).astype(BF16)
            q_swap, c_swap = pltpu.roll(q, 64, 1), pltpu.roll(c, 64, 1)
            q_rows = (jnp.where(low, q, 0.0).astype(BF16), jnp.where(low, q_swap, 0.0).astype(BF16))
            c_rows = (jnp.where(low, 0.0, c_swap).astype(BF16), jnp.where(low, 0.0, c).astype(BF16))
            for side in range(2):
                g = pair * 2 + side
                for part in range(2):
                    toks = slice(part * 128, part * 128 + 128)
                    lanes = slice(g * 128, g * 128 + 128)
                    q_t[j, part, 0:64, lanes] = q_turn[side * 64 : side * 64 + 64, toks]
                    c_t[j, part, 64:128, lanes] = c_turn[side * 64 : side * 64 + 64, toks]
                    q_n[j, part, lanes, :] = q_rows[side][toks, :]
                    c_n[j, part, lanes, :] = c_rows[side][toks, :]

    def forward(j, carry):
        for k in NEAR:
            wait_y(j, k)
            for a in (2, 1, 3):
                copy_x(j, (y + NY - k) % NY, a).start()
        return carry

    lax.fori_loop(0, CH, forward, 0)

    ins[4].wait()
    seg_i = jnp.broadcast_to(seg[...].astype(F32), (TOK, TOK))
    seg_j = jnp.transpose(seg_i)
    pos_j = lax.broadcasted_iota(jnp.int32, (TOK, TOK), 0)
    pos_i = lax.broadcasted_iota(jnp.int32, (TOK, TOK), 1)
    bias = jnp.where((seg_i == seg_j) & (pos_i >= pos_j), 0.0, -1e30)
    bias_a[...] = bias[0:128, 0:128]
    bias_b[...] = bias[:, 128:256]

    def wait_x(j):
        pltpu.make_async_copy(w.at[j, core, 0:3], w.at[j, core, 0:3], ax_r.at[j]).wait()

    def other_core():
        return at(x, y, z, 1 - core)

    def copy_core(j):
        return pltpu.make_async_remote_copy(
            w.at[j, core], w.at[j, core], ac_s, ac_r.at[j],
            device_id=other_core(), device_id_type=MESH,
        )

    def wait_core(j):
        pltpu.make_async_copy(w.at[j, 1 - core], w.at[j, 1 - core], ac_r.at[j]).wait()

    wait_x(0)
    copy_core(0).start()

    def heads(s_ref, d_ref, b_ref, p_ref, o_ref):
        def one(g, carry):
            lanes = pl.ds(pl.multiple_of(g * 128, 128), 128)
            s = s_ref[:, lanes] + b_ref[...]
            e = jnp.exp(s - jnp.max(s, axis=0, keepdims=True))
            p = e * (1.0 / jnp.sum(e, axis=0, keepdims=True))
            pb = p.astype(BF16)
            d = d_ref[:, lanes]
            delta = jnp.sum(pb.astype(F32) * d, axis=0, keepdims=True)
            p_ref[:, lanes] = pb
            o_ref[:, lanes] = (p * (d - delta)).astype(BF16)
            return carry

        lax.fori_loop(0, GROUP, one, 0)

    def copy_rc(j):
        return pltpu.make_async_remote_copy(
            g_send.at[j], c_recv.at[j], rc_s, rc_r.at[j],
            device_id=other_core(), device_id_type=MESH,
        )

    def copy_rx(j, a):
        to = (x + a) % NX
        return pltpu.make_async_remote_copy(
            x_send.at[j, to], x_recv.at[j, a - 1], rx_s, rx_r.at[j],
            device_id=at(to, y, z, core), device_id_type=MESH,
        )

    def copy_ry(j, k):
        to = (y + k) % NY
        return pltpu.make_async_remote_copy(
            y_send.at[j, to], y_recv.at[j, k - 1], ry_s, ry_r.at[j],
            device_id=at(x, to, z, core), device_id_type=MESH,
        )

    def take_x(j):
        pltpu.make_async_copy(x_recv.at[j], x_recv.at[j], rx_r.at[j]).wait()
        total = x_send[j, x].astype(F32)
        for a in range(NX - 1):
            total += x_recv[j, a].astype(F32)
        y_send[j] = total.astype(BF16)
        for k in (4, 3, 5, 2, 6, 1, 7):
            copy_ry(j, k).start()

    def take_y(j):
        pltpu.make_async_copy(y_recv.at[j], y_recv.at[j], ry_r.at[j]).wait()
        total = y_send[j, y].astype(F32)
        for k in range(NY - 1):
            total += y_recv[j, k].astype(F32)
        z_sum[j] = total.astype(BF16)

    def chunk(j, carry):
        wait_core(j)
        kv = jnp.zeros((TOK, 128), F32)
        for xx in range(NX):
            kv += dot(hid[:, xx * 512 : (xx + 1) * 512], natural(w, j, xx))
        kv = kv.astype(BF16)
        s_a[...] = dot(kv[0:128], q_t[j, 0])
        d_a[...] = dot(kv[0:128], c_t[j, 0])
        s_b[...] = dot(kv, q_t[j, 1])
        d_b[...] = dot(kv, c_t[j, 1])
        heads(s_a, d_a, bias_a, p_a, ds_a)
        heads(s_b, d_b, bias_b, p_b, ds_b)
        late = dot(ds_b[...], q_n[j, 1]) + dot(p_b[...], c_n[j, 1])
        early = dot(ds_a[...], q_n[j, 0]) + dot(p_a[...], c_n[j, 0])
        grad = jnp.concatenate([late[0:128] + early, late[128:256]], axis=0).astype(BF16)
        gkv[j] = grad
        g_send[j] = dot(h_t[1 - core], grad).astype(BF16).reshape(NX, NY, 32, 128)
        copy_rc(j).start()

        @pl.when(j < CH - 1)
        def _():
            wait_x(j + 1)
            copy_core(j + 1).start()

        @pl.when(j >= 2)
        def _():
            take_x(j - 2)

        pltpu.make_async_copy(c_recv.at[j], c_recv.at[j], rc_r.at[j]).wait()
        part = dot(h_t[core], gkv[j]).reshape(NX, NY, 32, 128) + c_recv[j].astype(F32)
        x_send[j] = part.astype(BF16)
        for a in (2, 1, 3):
            copy_rx(j, a).start()
        return carry

    lax.fori_loop(0, CH, chunk, 0)

    take_x(CH - 2)
    grads = jnp.concatenate([gkv[j] for j in range(CH)], axis=1)

    def hidden_part(xx, carry):
        rows = jnp.concatenate([natural(w, j, xx) for j in range(CH)], axis=1)
        cols = pl.ds(pl.multiple_of(xx * 512, 512), 512)
        gh[:, cols] = lax.dot_general(grads, rows, NT, preferred_element_type=F32).astype(BF16)
        return carry

    lax.fori_loop(0, NX, hidden_part, 0)
    out = pltpu.make_async_copy(gh, gh_hbm, out_sem)
    out.start()

    take_x(CH - 1)
    lax.fori_loop(0, CH, lambda j, carry: (take_y(j), carry)[1], 0)

    back = ((r_out % 16) // 4) * 32 + (r_out // 16) * 4 + r_out % 4
    z_send[...] = (
        dot((r_in == back).astype(BF16), z_sum[...].reshape(128, 128)).astype(BF16).reshape(8, 16, 128)
    )

    def scatter_z(a, b, remote):
        to_h, to_c = (zh + a) % NZH, (core + b) % NC
        piece = z_send.at[to_h * NC + to_c]
        if not remote:
            return pltpu.make_async_copy(piece, f_recv.at[z], rz_r)
        return pltpu.make_async_remote_copy(
            piece, f_recv.at[z], rz_s, rz_r,
            device_id=at(x, y, to_h * NZL + core, to_c), device_id_type=MESH,
        )

    for a in (2, 1, 3, 0):
        for b in range(NC):
            if a or b:
                scatter_z(a, b, True).start()

    @pl.when(home)
    def _():
        scatter_z(0, 0, False).start()

    @pl.when(jnp.logical_not(home))
    def _():
        scatter_z(0, 0, True).start()

    pltpu.make_async_copy(zrecv.at[0:7], zrecv.at[0:7], az_s).wait()

    @pl.when(jnp.logical_not(home))
    def _():
        pltpu.make_async_copy(zrecv.at[0], zrecv.at[0], az_s).wait()

    pltpu.make_async_copy(y_recv, y_recv, ay_s).wait()
    pltpu.make_async_copy(x_recv, x_recv, ax_s).wait()
    pltpu.make_async_copy(c_recv, c_recv, ac_s).wait()
    pltpu.make_async_copy(c_recv, c_recv, rc_s).wait()
    pltpu.make_async_copy(x_recv, x_recv, rx_s).wait()
    pltpu.make_async_copy(y_recv, y_recv, ry_s).wait()
    out.wait()

    pltpu.make_async_copy(f_recv, f_recv, rz_r).wait()
    total = f_recv[0].astype(F32)
    for k in range(1, 8):
        total += f_recv[k].astype(F32)
    gw_ref[...] = total * scale

    pltpu.make_async_copy(f_recv.at[0:7], f_recv.at[0:7], rz_s).wait()

    @pl.when(jnp.logical_not(home))
    def _():
        pltpu.make_async_copy(f_recv.at[0], f_recv.at[0], rz_s).wait()


def on_device(hidden, queries, cotangent, segments, kv_weight):
    any_space = pl.BlockSpec(memory_space=pl.ANY)
    vmem = pl.BlockSpec(memory_space=pltpu.VMEM)
    scale = 1.0 / math.sqrt(lax.axis_size(("dp", "node")) * TOK)
    dma = pltpu.SemaphoreType.DMA
    scratch = [
        ((TOK, 2048), BF16), ((TOK, 1024), BF16), ((TOK, 1024), BF16), ((1, TOK), jnp.int32), ((4, 512), BF16),
        ((16, 128), BF16), ((8, 16, 128), BF16), ((CH, 2, NX, NY, 32, 128), BF16), ((2, 1024, TOK), BF16),
        ((CH, 2, 128, 512), BF16), ((CH, 2, 128, 512), BF16), ((CH, 2, 512, 128), BF16), ((CH, 2, 512, 128), BF16),
        ((128, 128), F32), ((256, 128), F32),
        ((128, 512), F32), ((256, 512), F32), ((128, 512), F32), ((256, 512), F32),
        ((128, 512), BF16), ((256, 512), BF16), ((128, 512), BF16), ((256, 512), BF16), ((CH, TOK, 128), BF16),
        ((CH, NX, NY, 32, 128), BF16), ((CH, NX, NY, 32, 128), BF16),
        ((CH, NX, NY, 32, 128), BF16), ((CH, NX - 1, NY, 32, 128), BF16),
        ((CH, NY, 32, 128), BF16), ((CH, NY - 1, 32, 128), BF16),
        ((CH, 32, 128), BF16), ((8, 16, 128), BF16), ((8, 16, 128), BF16), ((TOK, 2048), BF16),
    ]
    grad_hidden, packed = pl.pallas_call(
        functools.partial(kernel, scale),
        out_shape=(
            jax.ShapeDtypeStruct((TOK, 2048), BF16),
            jax.ShapeDtypeStruct((16, 128), F32),
        ),
        in_specs=[any_space] * 5,
        out_specs=(any_space, vmem),
        scratch_shapes=[pltpu.VMEM(shape, kind) for shape, kind in scratch]
        + [
            dma((5,)), dma,
            dma, dma, dma, dma((CH, NY - 1)), dma, dma((CH,)), dma, dma((CH,)),
            dma, dma((CH,)), dma, dma((CH,)), dma, dma((CH,)), dma, dma,
        ],
        compiler_params=pltpu.CompilerParams(
            collective_id=0, has_side_effects=True, vmem_limit_bytes=48 << 20
        ),
    )(hidden, queries, cotangent, segments, kv_weight)
    grad_weights = packed.reshape(CH, 4, 2, 64).transpose(1, 2, 0, 3).reshape(4, 512)
    return grad_hidden, grad_weights


def solution(mesh):
    placed = P(("dp", "node"), None)
    return jax.shard_map(
        on_device,
        mesh=mesh,
        in_specs=(placed,) * 5,
        out_specs=(placed, placed),
        check_vma=False,
    )
```

time: 1130 us -> 70.6 us (0.06)
  waiting for transfers between devices: 1080 us -> 0 us
  Pallas kernels: 0 us -> 63.2 us
  matrix products: 16.5 us -> 0 us
  between operations: 13.8 us -> 0.65 us
    all_gather x2 -> x0, waiting for transfers between devices: 801 us -> none  [the longest x1 763 us: on_device(): full_weight = lax.all_gather(kv_weight, ('dp', 'node'), axis=0, tiled=True)]
    unnamed x4 -> x0, waiting for transfers between devices: 279 us -> none
    pallas_call x0 -> x1, Pallas kernels: none -> 63.2 us  [on_device(): pl.pallas_call(functools.partial(kernel, scale), out_shape=(jax.ShapeDtyp...]
    dot_general x6 -> x0, matrix products: 13.1 us -> none  [the longest x1 3.58 us: attend_backward(): jnp.einsum('hgqk,qhgd->khd', grad_scores, query_heads, preferred_element_...]
  transfers between devices with their start and end apart: 3 -> 0, of which waited for: 3 -> 0; matrix products, arithmetic and copies ran while one was open for 1% -> 0% of each run, Pallas kernels for 0% -> 0%
where the time goes in v1:
time: 70.6 us; the launch traced here: 70.3 us
  Pallas kernels  63.2 us (90%)
  local copies, waits for them, and re-layouts  6.41 us (9%)
    pallas_call x1, Pallas kernels, on_device(): pl.pallas_call(functools.partial(kernel, scale), out_shape=(jax.ShapeDtyp...  63.2 us
    unnamed x11, local copies, waits for them, and re-layouts  5.63 us

profile of v1, /device:TPU:1, one launch (start us, length us, event | category | flops | bytes accessed | tf_op | source)
XLA Modules:
  0.0 70.3 jit_solution(14877838141761017204)
XLA Ops:
  0.6 0.0 copy-start
  0.6 1.2 %copy-done = bf16[256,2048]{1,0:T(8,128)(2,1)S(1)} copy-done((bf16[256,2048]{1,0:T(8,128)(2,1)S(1)}, bf16[256,2048]{1,0:T(8,128)(2,1)}, u32[]{:S(2)}) %copy-start) | copy-done | bytes 1048600
  1.9 0.0 copy-start.1
  1.9 1.0 %copy-done.1 = bf16[256,1024]{1,0:T(8,128)(2,1)S(1)} copy-done((bf16[256,1024]{1,0:T(8,128)(2,1)S(1)}, bf16[256,1024]{1,0:T(8,128)(2,1)}, u32[]{:S(2)}) %copy-start.1) | copy-done | bytes 524312
  2.9 0.0 copy-start.2
  2.9 1.0 %copy-done.2 = bf16[256,1024]{1,0:T(8,128)(2,1)S(1)} copy-done((bf16[256,1024]{1,0:T(8,128)(2,1)S(1)}, bf16[256,1024]{1,0:T(8,128)(2,1)}, u32[]{:S(2)}) %copy-start.2) | copy-done | bytes 524312
  3.9 0.0 copy-start.3
  3.9 0.7 copy-done.3
  4.6 0.0 copy-start.4
  4.6 0.7 copy-done.4
  5.3 63.2 %shard_map.68 = (bf16[256,2048]{1,0:T(8,128)(2,1)S(1)}, f32[16,128]{1,0:T(8,128)S(1)}) custom-call(bf16[256,2048]{1,0:T(8,128)(2,1)S(1)} %copy-done, bf16[256,1024]{1,0:T(8,128)(2,1)S(1)} %copy-done.1, bf16[256,1024]{1,0:T(8,128)(2,1)S(1)} %copy-done.2, s32[1,256]{1,0:T(1,128)S(1)} %copy-done.4, bf16[4,512]{1,0:T(4,128)(2,1)S(1)} %copy-done.3), custom_call_target="tpu_custom_call" | custom-call | tf_op jit(solution)/shard_map/pallas_call | solution.py:408
  68.5 0.1 reshape.10
  68.6 0.7 reshape.11
  69.3 1.0 %copy.9 = bf16[256,2048]{1,0:T(8,128)(2,1)} copy(bf16[256,2048]{1,0:T(8,128)(2,1)S(1)} %get-tuple-element.8) | data formatting | bytes 2097152
  (1 shorter events, 0.0 us)
Async XLA Ops:
  0.6 1.2 %copy-start = (bf16[256,2048]{1,0:T(8,128)(2,1)S(1)}, bf16[256,2048]{1,0:T(8,128)(2,1)}, u32[]{:S(2)}) copy-start(bf16[256,2048]{1,0:T(8,128)(2,1)} %hid_hbm.1) | copy-start | bytes 3145732
  1.9 1.0 %copy-start.1 = (bf16[256,1024]{1,0:T(8,128)(2,1)S(1)}, bf16[256,1024]{1,0:T(8,128)(2,1)}, u32[]{:S(2)}) copy-start(bf16[256,1024]{1,0:T(8,128)(2,1)} %que_hbm.1) | copy-start | bytes 1572868
  2.9 1.0 %copy-start.2 = (bf16[256,1024]{1,0:T(8,128)(2,1)S(1)}, bf16[256,1024]{1,0:T(8,128)(2,1)}, u32[]{:S(2)}) copy-start(bf16[256,1024]{1,0:T(8,128)(2,1)} %cot_hbm.1) | copy-start | bytes 1572868
  3.9 0.7 copy-start.3
  4.6 0.7 copy-start.4

commit v2 on v1

--- a/solution.py
+++ b/solution.py
@@ -20,6 +20,8 @@
 F32, BF16 = jnp.float32, jnp.bfloat16
 NT = (((1,), (1,)), ((), ()))
 NEAR = (1, 7, 2, 6, 3, 5, 4)
+FAR = (4, 3, 5, 2, 6, 1, 7, 0)
+LAST = CH - 1
 
 
 def dot(a, b):
@@ -40,7 +42,7 @@
     s_a, s_b, d_a, d_b, p_a, p_b, ds_a, ds_b, gkv,
     g_send, c_recv, x_send, x_recv, y_send, y_recv, z_sum, z_send, f_recv, gh,
     in_sem, out_sem,
-    az_s, az_r, ay_s, ay_r, ax_s, ax_r, ac_s, ac_r,
+    az_s, az_r, ay_s, ay_r, ax_s, ax_r, bx_s, bx_r, by_s, by_r, ac_s, ac_r,
     rc_s, rc_r, rx_s, rx_r, ry_s, ry_r, rz_s, rz_r,
 ):
     dp, node = lax.axis_index("dp"), lax.axis_index("node")
@@ -145,6 +147,24 @@
             device_id=at(x, (y + k) % NY, z, core), device_id_type=MESH,
         )
 
+    def first_x(a):
+        return pltpu.make_async_remote_copy(
+            w.at[LAST, core, x, y], w.at[LAST, core, x, y], bx_s, bx_r.at[a - 1],
+            device_id=at((x + a) % NX, y, z, core), device_id_type=MESH,
+        )
+
+    def wait_first_x(a):
+        src = (x + NX - a) % NX
+        pltpu.make_async_copy(
+            w.at[LAST, core, src, y], w.at[LAST, core, src, y], bx_r.at[a - 1]
+        ).wait()
+
+    def then_y(xb, k):
+        return pltpu.make_async_remote_copy(
+            w.at[LAST, core, xb, y], w.at[LAST, core, xb, y], by_s, by_r,
+            device_id=at(x, (y + k) % NY, z, core), device_id_type=MESH,
+        )
+
     def wait_y(j, k):
         src = (y + NY - k) % NY
         pltpu.make_async_copy(
@@ -164,7 +184,12 @@
             copy_x(j, y, a).start()
         return carry
 
-    lax.fori_loop(0, CH, send_y, 0)
+    lax.fori_loop(0, 1, send_y, 0)
+    for a in (2, 1, 3):
+        first_x(a).start()
+    lax.fori_loop(1, LAST, send_y, 0)
+    for k in NEAR:
+        then_y(x, k).start()
 
     ins[2].wait()
     ins[3].wait()
@@ -200,7 +225,12 @@
                 copy_x(j, (y + NY - k) % NY, a).start()
         return carry
 
-    lax.fori_loop(0, CH, forward, 0)
+    lax.fori_loop(0, 1, forward, 0)
+    for a in (1, 3, 2):
+        wait_first_x(a)
+        for k in NEAR:
+            then_y((x + NX - a) % NX, k).start()
+    lax.fori_loop(1, LAST, forward, 0)
 
     ins[4].wait()
     seg_i = jnp.broadcast_to(seg[...].astype(F32), (TOK, TOK))
@@ -214,6 +244,10 @@
     def wait_x(j):
         pltpu.make_async_copy(w.at[j, core, 0:3], w.at[j, core, 0:3], ax_r.at[j]).wait()
 
+    def wait_then_y():
+        blocks = w.at[LAST, core, :, 0 : NY - 1]
+        pltpu.make_async_copy(blocks, blocks, by_r).wait()
+
     def other_core():
         return at(x, y, z, 1 - core)
 
@@ -230,8 +264,8 @@
     copy_core(0).start()
 
     def heads(s_ref, d_ref, b_ref, p_ref, o_ref):
-        def one(g, carry):
-            lanes = pl.ds(pl.multiple_of(g * 128, 128), 128)
+        for g in range(GROUP):
+            lanes = slice(g * 128, g * 128 + 128)
             s = s_ref[:, lanes] + b_ref[...]
             e = jnp.exp(s - jnp.max(s, axis=0, keepdims=True))
             p = e * (1.0 / jnp.sum(e, axis=0, keepdims=True))
@@ -240,9 +274,6 @@
             delta = jnp.sum(pb.astype(F32) * d, axis=0, keepdims=True)
             p_ref[:, lanes] = pb
             o_ref[:, lanes] = (p * (d - delta)).astype(BF16)
-            return carry
-
-        lax.fori_loop(0, GROUP, one, 0)
 
     def copy_rc(j):
         return pltpu.make_async_remote_copy(
@@ -250,10 +281,10 @@
             device_id=other_core(), device_id_type=MESH,
         )
 
-    def copy_rx(j, a):
-        to = (x + a) % NX
-        return pltpu.make_async_remote_copy(
-            x_send.at[j, to], x_recv.at[j, a - 1], rx_s, rx_r.at[j],
+    def copy_rx(j, k, a):
+        to, yb = (x + a) % NX, (y + k) % NY
+        return pltpu.make_async_remote_copy(
+            x_send.at[j, to, yb], x_recv.at[j, a - 1, yb], rx_s, rx_r.at[j, k],
             device_id=at(to, y, z, core), device_id_type=MESH,
         )
 
@@ -265,13 +296,16 @@
         )
 
     def take_x(j):
-        pltpu.make_async_copy(x_recv.at[j], x_recv.at[j], rx_r.at[j]).wait()
-        total = x_send[j, x].astype(F32)
-        for a in range(NX - 1):
-            total += x_recv[j, a].astype(F32)
-        y_send[j] = total.astype(BF16)
-        for k in (4, 3, 5, 2, 6, 1, 7):
-            copy_ry(j, k).start()
+        for k in FAR:
+            yb = (y + k) % NY
+            blocks = x_recv.at[j, :, yb]
+            pltpu.make_async_copy(blocks, blocks, rx_r.at[j, k]).wait()
+            total = x_send[j, x, yb].astype(F32)
+            for a in range(NX - 1):
+                total += x_recv[j, a, yb].astype(F32)
+            y_send[j, yb] = total.astype(BF16)
+            if k:
+                copy_ry(j, k).start()
 
     def take_y(j):
         pltpu.make_async_copy(y_recv.at[j], y_recv.at[j], ry_r.at[j]).wait()
@@ -292,6 +326,17 @@
         d_b[...] = dot(kv, c_t[j, 1])
         heads(s_a, d_a, bias_a, p_a, ds_a)
         heads(s_b, d_b, bias_b, p_b, ds_b)
+
+        @pl.when(j < LAST - 1)
+        def _():
+            wait_x(j + 1)
+            copy_core(j + 1).start()
+
+        @pl.when(j == LAST - 1)
+        def _():
+            wait_then_y()
+            copy_core(LAST).start()
+
         late = dot(ds_b[...], q_n[j, 1]) + dot(p_b[...], c_n[j, 1])
         early = dot(ds_a[...], q_n[j, 0]) + dot(p_a[...], c_n[j, 0])
         grad = jnp.concatenate([late[0:128] + early, late[128:256]], axis=0).astype(BF16)
@@ -299,11 +344,6 @@
         g_send[j] = dot(h_t[1 - core], grad).astype(BF16).reshape(NX, NY, 32, 128)
         copy_rc(j).start()
 
-        @pl.when(j < CH - 1)
-        def _():
-            wait_x(j + 1)
-            copy_core(j + 1).start()
-
         @pl.when(j >= 2)
         def _():
             take_x(j - 2)
@@ -311,8 +351,9 @@
         pltpu.make_async_copy(c_recv.at[j], c_recv.at[j], rc_r.at[j]).wait()
         part = dot(h_t[core], gkv[j]).reshape(NX, NY, 32, 128) + c_recv[j].astype(F32)
         x_send[j] = part.astype(BF16)
-        for a in (2, 1, 3):
-            copy_rx(j, a).start()
+        for k in FAR:
+            for a in (2, 1, 3):
+                copy_rx(j, k, a).start()
         return carry
 
     lax.fori_loop(0, CH, chunk, 0)
@@ -367,8 +408,12 @@
     def _():
         pltpu.make_async_copy(zrecv.at[0], zrecv.at[0], az_s).wait()
 
-    pltpu.make_async_copy(y_recv, y_recv, ay_s).wait()
-    pltpu.make_async_copy(x_recv, x_recv, ax_s).wait()
+    ay_all, ax_all = y_recv.at[0:LAST], x_recv.at[0:LAST]
+    pltpu.make_async_copy(ay_all, ay_all, ay_s).wait()
+    pltpu.make_async_copy(ax_all, ax_all, ax_s).wait()
+    bx_all, by_all = x_recv.at[0, :, 0], c_recv.at[0, :, 0 : NY - 1]
+    pltpu.make_async_copy(bx_all, bx_all, bx_s).wait()
+    pltpu.make_async_copy(by_all, by_all, by_s).wait()
     pltpu.make_async_copy(c_recv, c_recv, ac_s).wait()
     pltpu.make_async_copy(c_recv, c_recv, rc_s).wait()
     pltpu.make_async_copy(x_recv, x_recv, rx_s).wait()
@@ -416,11 +461,11 @@
         scratch_shapes=[pltpu.VMEM(shape, kind) for shape, kind in scratch]
         + [
             dma((5,)), dma,
-            dma, dma, dma, dma((CH, NY - 1)), dma, dma((CH,)), dma, dma((CH,)),
-            dma, dma((CH,)), dma, dma((CH,)), dma, dma((CH,)), dma, dma,
+            dma, dma, dma, dma((LAST, NY - 1)), dma, dma((LAST,)), dma, dma((NX - 1,)), dma, dma, dma, dma((CH,)),
+            dma, dma((CH,)), dma, dma((CH, NY)), dma, dma((CH,)), dma, dma,
         ],
         compiler_params=pltpu.CompilerParams(
-            collective_id=0, has_side_effects=True, vmem_limit_bytes=48 << 20
+            collective_id=0, has_side_effects=True, vmem_limit_bytes=62 << 20
         ),
     )(hidden, queries, cotangent, segments, kv_weight)
     grad_weights = packed.reshape(CH, 4, 2, 64).transpose(1, 2, 0, 3).reshape(4, 512)

time: 70.6 us -> 63.5 us (0.90)
  Pallas kernels: 63.2 us -> 58.9 us
  local copies, waits for them, and re-layouts: 6.41 us -> 3.77 us
    pallas_call x1, Pallas kernels: 63.2 us -> 58.9 us  [on_device(): pl.pallas_call(functools.partial(kernel, scale), out_shape=(jax.ShapeDtyp...]
    unnamed x11 -> x1, local copies, waits for them, and re-layouts: 5.63 us -> 2.3 us
where the time goes in v2:
time: 63.5 us; the launch traced here: 63.3 us
  Pallas kernels  58.9 us (93%)
  local copies, waits for them, and re-layouts  3.77 us (6%)
  between operations  0.64 us (1%)
    pallas_call x1, Pallas kernels, on_device(): pl.pallas_call(functools.partial(kernel, scale), out_shape=(jax.ShapeDtyp...  58.9 us
    unnamed x1, local copies, waits for them, and re-layouts  2.3 us
    reshape x2, local copies, waits for them, and re-layouts, on_device(): packed.reshape(CH, 4, 2, 64).transpose(1, 2, 0, 3).reshape(4, 512)  1.46 us

profile of v2, /device:TPU:1, one launch (start us, length us, event | category | flops | bytes accessed | tf_op | source)
XLA Modules:
  0.0 63.3 jit_solution(10859457086998985858)
XLA Ops:
  0.6 58.9 %shard_map.68 = (bf16[256,2048]{1,0:T(8,128)(2,1)}, f32[16,128]{1,0:T(8,128)}) custom-call(bf16[256,2048]{1,0:T(8,128)(2,1)} %hid_hbm.1, bf16[256,1024]{1,0:T(8,128)(2,1)} %que_hbm.1, bf16[256,1024]{1,0:T(8,128)(2,1)} %cot_hbm.1, s32[1,256]{1,0:T(1,128)} %seg_hbm.1, bf16[4,512]{1,0:T(4,128)(2,1)} %kvw_hbm.1), custom_call_target="tpu_custom_call" | custom-call | tf_op jit(solution)/shard_map/pallas_call | solution.py:453
  59.5 0.8 %reshape.10 = f32[4,4,2,64]{3,2,1,0:T(2,128)S(1)} reshape(f32[16,128]{1,0:T(8,128)} %get-tuple-element.5) | data formatting | bytes 16384 | tf_op jit(solution)/shard_map/reshape | solution.py:471
  60.3 0.7 %reshape.11 = f32[4,512]{1,0:T(4,128)} reshape(f32[4,2,4,64]{3,2,1,0:T(4,128)S(1)} %copy.7) | data formatting | bytes 16384 | tf_op jit(solution)/shard_map/reshape | solution.py:471
  61.0 2.3 %copy.9 = bf16[256,2048]{1,0:T(8,128)(2,1)} copy(bf16[256,2048]{1,0:T(8,128)(2,1)} %get-tuple-element.8) | data formatting | bytes 2097152
  (1 shorter events, 0.0 us)

commit v3 on v2

--- a/solution.py
+++ b/solution.py
@@ -56,6 +56,33 @@
     def at(x_, y_, z_, c_):
         return ((x_ * NY + y_) * NZL + z_ % NZL, (z_ // NZL) * NC + c_)
 
+    barrier = pltpu.get_barrier_semaphore()
+
+    def greet_z(k):
+        other = (z * NC + core + k) % NZC
+        pl.semaphore_signal(
+            barrier, inc=1, device_id=at(x, y, other // NC, other % NC), device_id_type=MESH
+        )
+
+    def greet_y(k):
+        pl.semaphore_signal(
+            barrier, inc=1, device_id=at(x, (y + k) % NY, z, core), device_id_type=MESH
+        )
+
+    def greet_x(k):
+        pl.semaphore_signal(
+            barrier, inc=1, device_id=at((x + k) % NX, y, z, core), device_id_type=MESH
+        )
+
+    for k in (8, 9, 7, 10, 6, 11, 5, 12, 4):
+        greet_z(k)
+    for k in FAR[:-1]:
+        greet_y(k)
+    for k in (13, 3, 14, 2, 15, 1):
+        greet_z(k)
+    for k in (2, 1, 3):
+        greet_x(k)
+
     ins = [
         pltpu.make_async_copy(kvw_hbm, kvw, in_sem.at[0]),
         pltpu.make_async_copy(hid_hbm, hid, in_sem.at[1]),
@@ -65,31 +92,6 @@
     ]
     for cp in ins:
         cp.start()
-
-    barrier = pltpu.get_barrier_semaphore()
-
-    def greet_z(k, carry):
-        other = (z * NC + core + k) % NZC
-        pl.semaphore_signal(
-            barrier, inc=1, device_id=at(x, y, other // NC, other % NC), device_id_type=MESH
-        )
-        return carry
-
-    def greet_y(k, carry):
-        pl.semaphore_signal(
-            barrier, inc=1, device_id=at(x, (y + k) % NY, z, core), device_id_type=MESH
-        )
-        return carry
-
-    def greet_x(k, carry):
-        pl.semaphore_signal(
-            barrier, inc=1, device_id=at((x + k) % NX, y, z, core), device_id_type=MESH
-        )
-        return carry
-
-    lax.fori_loop(1, NZC, greet_z, 0)
-    lax.fori_loop(1, NY, greet_y, 0)
-    lax.fori_loop(1, NX, greet_x, 0)
 
     ins[0].wait()
     own = kvw[...].astype(F32)
@@ -314,6 +316,14 @@
             total += y_recv[j, k].astype(F32)
         z_sum[j] = total.astype(BF16)
 
+    def both_cores(j):
+        pltpu.make_async_copy(c_recv.at[j], c_recv.at[j], rc_r.at[j]).wait()
+        part = dot(h_t[core], gkv[j]).reshape(NX, NY, 32, 128) + c_recv[j].astype(F32)
+        x_send[j] = part.astype(BF16)
+        for k in FAR:
+            for a in (2, 1, 3):
+                copy_rx(j, k, a).start()
+
     def chunk(j, carry):
         wait_core(j)
         kv = jnp.zeros((TOK, 128), F32)
@@ -324,6 +334,11 @@
         d_a[...] = dot(kv[0:128], c_t[j, 0])
         s_b[...] = dot(kv, q_t[j, 1])
         d_b[...] = dot(kv, c_t[j, 1])
+
+        @pl.when(j > 0)
+        def _():
+            both_cores(j - 1)
+
         heads(s_a, d_a, bias_a, p_a, ds_a)
         heads(s_b, d_b, bias_b, p_b, ds_b)
 
@@ -343,22 +358,14 @@
         gkv[j] = grad
         g_send[j] = dot(h_t[1 - core], grad).astype(BF16).reshape(NX, NY, 32, 128)
         copy_rc(j).start()
-
-        @pl.when(j >= 2)
-        def _():
-            take_x(j - 2)
-
-        pltpu.make_async_copy(c_recv.at[j], c_recv.at[j], rc_r.at[j]).wait()
-        part = dot(h_t[core], gkv[j]).reshape(NX, NY, 32, 128) + c_recv[j].astype(F32)
-        x_send[j] = part.astype(BF16)
-        for k in FAR:
-            for a in (2, 1, 3):
-                copy_rx(j, k, a).start()
         return carry
 
     lax.fori_loop(0, CH, chunk, 0)
 
-    take_x(CH - 2)
+    take_x(0)
+    both_cores(LAST)
+    take_x(1)
+    take_x(2)
     grads = jnp.concatenate([gkv[j] for j in range(CH)], axis=1)
 
     def hidden_part(xx, carry):
@@ -418,13 +425,16 @@
     pltpu.make_async_copy(c_recv, c_recv, rc_s).wait()
     pltpu.make_async_copy(x_recv, x_recv, rx_s).wait()
     pltpu.make_async_copy(y_recv, y_recv, ry_s).wait()
+
     out.wait()
-
     pltpu.make_async_copy(f_recv, f_recv, rz_r).wait()
     total = f_recv[0].astype(F32)
     for k in range(1, 8):
         total += f_recv[k].astype(F32)
-    gw_ref[...] = total * scale
+    total *= scale
+    gw_ref[...] = jnp.concatenate(
+        [total[4 * j : 4 * j + 4, side * 64 : side * 64 + 64] for side in range(2) for j in range(CH)], axis=1
+    )
 
     pltpu.make_async_copy(f_recv.at[0:7], f_recv.at[0:7], rz_s).wait()
 
@@ -434,7 +444,7 @@
 
 
 def on_device(hidden, queries, cotangent, segments, kv_weight):
-    any_space = pl.BlockSpec(memory_space=pl.ANY)
+    hbm = pl.BlockSpec(memory_space=pl.ANY)
     vmem = pl.BlockSpec(memory_space=pltpu.VMEM)
     scale = 1.0 / math.sqrt(lax.axis_size(("dp", "node")) * TOK)
     dma = pltpu.SemaphoreType.DMA
@@ -450,14 +460,14 @@
         ((CH, NY, 32, 128), BF16), ((CH, NY - 1, 32, 128), BF16),
         ((CH, 32, 128), BF16), ((8, 16, 128), BF16), ((8, 16, 128), BF16), ((TOK, 2048), BF16),
     ]
-    grad_hidden, packed = pl.pallas_call(
+    return pl.pallas_call(
         functools.partial(kernel, scale),
         out_shape=(
             jax.ShapeDtypeStruct((TOK, 2048), BF16),
-            jax.ShapeDtypeStruct((16, 128), F32),
+            jax.ShapeDtypeStruct((4, 512), F32),
         ),
-        in_specs=[any_space] * 5,
-        out_specs=(any_space, vmem),
+        in_specs=[hbm] * 5,
+        out_specs=(hbm, vmem),
         scratch_shapes=[pltpu.VMEM(shape, kind) for shape, kind in scratch]
         + [
             dma((5,)), dma,
@@ -468,8 +478,6 @@
             collective_id=0, has_side_effects=True, vmem_limit_bytes=62 << 20
         ),
     )(hidden, queries, cotangent, segments, kv_weight)
-    grad_weights = packed.reshape(CH, 4, 2, 64).transpose(1, 2, 0, 3).reshape(4, 512)
-    return grad_hidden, grad_weights
 
 
 def solution(mesh):

time: 63.5 us -> 60.6 us (0.954)
  Pallas kernels: 58.9 us -> 56.9 us
  local copies, waits for them, and re-layouts: 3.77 us -> 2.91 us
    pallas_call x1, Pallas kernels: 58.9 us -> 56.9 us  [on_device(): pl.pallas_call(functools.partial(kernel, scale), out_shape=(jax.ShapeDtyp...]
    reshape x2 -> x0, local copies, waits for them, and re-layouts: 1.46 us -> none  [on_device(): packed.reshape(CH, 4, 2, 64).transpose(1, 2, 0, 3).reshape(4, 512)]
    unnamed x1 -> x4, local copies, waits for them, and re-layouts: 2.3 us -> 2.91 us
where the time goes in v3:
time: 60.6 us; the launch traced here: 60.5 us
  Pallas kernels  56.9 us (94%)
  local copies, waits for them, and re-layouts  2.91 us (5%)
  between operations  0.65 us (1%)
    pallas_call x1, Pallas kernels, on_device(): pl.pallas_call(functools.partial(kernel, scale), out_shape=(jax.ShapeDtyp...  56.9 us
    unnamed x4, local copies, waits for them, and re-layouts  2.91 us

profile of v3, /device:TPU:1, one launch (start us, length us, event | category | flops | bytes accessed | tf_op | source)
XLA Modules:
  0.0 60.5 jit_solution(10246558382525459076)
XLA Ops:
  0.6 56.9 %shard_map.68 = (bf16[256,2048]{1,0:T(8,128)(2,1)}, f32[4,512]{1,0:T(4,128)}) custom-call(bf16[256,2048]{1,0:T(8,128)(2,1)} %hid_hbm.1, bf16[256,1024]{1,0:T(8,128)(2,1)} %que_hbm.1, bf16[256,1024]{1,0:T(8,128)(2,1)} %cot_hbm.1, s32[1,256]{1,0:T(1,128)} %seg_hbm.1, bf16[4,512]{1,0:T(4,128)(2,1)} %kvw_hbm.1), custom_call_target="tpu_custom_call" | custom-call | tf_op jit(solution)/shard_map/pallas_call | solution.py:463
  57.6 0.0 copy-start
  57.6 2.3 %copy.9 = bf16[256,2048]{1,0:T(8,128)(2,1)} copy(bf16[256,2048]{1,0:T(8,128)(2,1)} %get-tuple-element.4) | data formatting | bytes 2097152
  59.9 0.0 copy-done
  59.9 0.6 copy.10
Async XLA Ops:
  57.6 2.3 %copy-start = (f32[4,512]{1,0:T(4,128)S(1)}, f32[4,512]{1,0:T(4,128)}, u32[]{:S(2)}) copy-start(f32[4,512]{1,0:T(4,128)} %get-tuple-element.5) | copy-start | bytes 24580

commit v4 on v3

--- a/solution.py
+++ b/solution.py
@@ -475,9 +475,14 @@
             dma, dma((CH,)), dma, dma((CH, NY)), dma, dma((CH,)), dma, dma,
         ],
         compiler_params=pltpu.CompilerParams(
-            collective_id=0, has_side_effects=True, vmem_limit_bytes=62 << 20
+            collective_id=0, has_side_effects=True, vmem_limit_bytes=40 << 20
         ),
-    )(hidden, queries, cotangent, segments, kv_weight)
+    )(
+        *(
+            pltpu.with_memory_space_constraint(array, pltpu.HBM)
+            for array in (hidden, queries, cotangent, segments, kv_weight)
+        )
+    )
 
 
 def solution(mesh):

time: 60.6 us -> 58.7 us (0.969)
  local copies, waits for them, and re-layouts: 2.91 us -> 1.57 us
    unnamed x4 -> x2, local copies, waits for them, and re-layouts: 2.91 us -> 1.57 us
where the time goes in v4:
time: 58.7 us; the launch traced here: 58.6 us
  Pallas kernels  56.4 us (96%)
  local copies, waits for them, and re-layouts  1.57 us (3%)
  between operations  0.64 us (1%)
    pallas_call x1, Pallas kernels, on_device(): pl.pallas_call(functools.partial(kernel, scale), out_shape=(jax.ShapeDtyp...  56.4 us
    unnamed x2, local copies, waits for them, and re-layouts  1.57 us

profile of v4, /device:TPU:1, one launch (start us, length us, event | category | flops | bytes accessed | tf_op | source)
XLA Modules:
  0.0 58.6 jit_solution(5868230178646997585)
XLA Ops:
  0.6 56.4 %shard_map.68 = (bf16[256,2048]{1,0:T(8,128)(2,1)S(1)}, f32[4,512]{1,0:T(4,128)S(1)}) custom-call(bf16[256,2048]{1,0:T(8,128)(2,1)} %hid_hbm.1, bf16[256,1024]{1,0:T(8,128)(2,1)} %que_hbm.1, bf16[256,1024]{1,0:T(8,128)(2,1)} %cot_hbm.1, s32[1,256]{1,0:T(1,128)} %seg_hbm.1, bf16[4,512]{1,0:T(4,128)(2,1)} %kvw_hbm.1), custom_call_target="tpu_custom_call" | custom-call | tf_op jit(solution)/shard_map/pallas_call | solution.py:463
  57.0 1.0 %copy.9 = bf16[256,2048]{1,0:T(8,128)(2,1)} copy(bf16[256,2048]{1,0:T(8,128)(2,1)S(1)} %get-tuple-element.4) | data formatting | bytes 2097152
  58.0 0.6 %copy.10 = f32[4,512]{1,0:T(4,128)} copy(f32[4,512]{1,0:T(4,128)S(1)} %get-tuple-element.5) | data formatting | bytes 16384

commit v5 on v4

--- a/solution.py
+++ b/solution.py
@@ -56,6 +56,15 @@
     def at(x_, y_, z_, c_):
         return ((x_ * NY + y_) * NZL + z_ % NZL, (z_ // NZL) * NC + c_)
 
+    ins = [
+        pltpu.make_async_copy(kvw_hbm, kvw, in_sem.at[0]),
+        pltpu.make_async_copy(hid_hbm, hid, in_sem.at[1]),
+        pltpu.make_async_copy(que_hbm, que, in_sem.at[2]),
+        pltpu.make_async_copy(cot_hbm, cot, in_sem.at[3]),
+        pltpu.make_async_copy(seg_hbm, seg, in_sem.at[4]),
+    ]
+    ins[0].start()
+
     barrier = pltpu.get_barrier_semaphore()
 
     def greet_z(k):
@@ -83,14 +92,7 @@
     for k in (2, 1, 3):
         greet_x(k)
 
-    ins = [
-        pltpu.make_async_copy(kvw_hbm, kvw, in_sem.at[0]),
-        pltpu.make_async_copy(hid_hbm, hid, in_sem.at[1]),
-        pltpu.make_async_copy(que_hbm, que, in_sem.at[2]),
-        pltpu.make_async_copy(cot_hbm, cot, in_sem.at[3]),
-        pltpu.make_async_copy(seg_hbm, seg, in_sem.at[4]),
-    ]
-    for cp in ins:
+    for cp in ins[1:]:
         cp.start()
 
     ins[0].wait()

time: 58.7 us -> 58.8 us (level)
  no operation moved by 1% of the time
where the time goes in v5:
time: 58.8 us; the launch traced here: 58.6 us
  Pallas kernels  56.4 us (96%)
  local copies, waits for them, and re-layouts  1.57 us (3%)
  between operations  0.64 us (1%)
    pallas_call x1, Pallas kernels, on_device(): pl.pallas_call(functools.partial(kernel, scale), out_shape=(jax.ShapeDtyp...  56.4 us
    unnamed x2, local copies, waits for them, and re-layouts  1.57 us

profile of v5, /device:TPU:1, one launch (start us, length us, event | category | flops | bytes accessed | tf_op | source)
XLA Modules:
  0.0 58.6 jit_solution(16851703801449990493)
XLA Ops:
  0.6 56.4 %shard_map.68 = (bf16[256,2048]{1,0:T(8,128)(2,1)S(1)}, f32[4,512]{1,0:T(4,128)S(1)}) custom-call(bf16[256,2048]{1,0:T(8,128)(2,1)} %hid_hbm.1, bf16[256,1024]{1,0:T(8,128)(2,1)} %que_hbm.1, bf16[256,1024]{1,0:T(8,128)(2,1)} %cot_hbm.1, s32[1,256]{1,0:T(1,128)} %seg_hbm.1, bf16[4,512]{1,0:T(4,128)(2,1)} %kvw_hbm.1), custom_call_target="tpu_custom_call" | custom-call | tf_op jit(solution)/shard_map/pallas_call | solution.py:465
  57.0 1.0 %copy.9 = bf16[256,2048]{1,0:T(8,128)(2,1)} copy(bf16[256,2048]{1,0:T(8,128)(2,1)S(1)} %get-tuple-element.4) | data formatting | bytes 2097152
  58.0 0.6 %copy.10 = f32[4,512]{1,0:T(4,128)} copy(f32[4,512]{1,0:T(4,128)S(1)} %get-tuple-element.5) | data formatting | bytes 16384

commit v6 on v4

--- a/solution.py
+++ b/solution.py
@@ -36,12 +36,12 @@
 def kernel(
     scale,
     hid_hbm, que_hbm, cot_hbm, seg_hbm, kvw_hbm,
-    gh_hbm, gw_ref,
+    gh, gw_ref,
     hid, que, cot, seg, kvw,
     blk, zrecv, w, h_t, q_t, c_t, q_n, c_n, bias_a, bias_b,
     s_a, s_b, d_a, d_b, p_a, p_b, ds_a, ds_b, gkv,
-    g_send, c_recv, x_send, x_recv, y_send, y_recv, z_sum, z_send, f_recv, gh,
-    in_sem, out_sem,
+    g_send, c_recv, x_send, x_recv, y_send, y_recv, z_sum, z_send, f_recv,
+    in_sem,
     az_s, az_r, ay_s, ay_r, ax_s, ax_r, bx_s, bx_r, by_s, by_r, ac_s, ac_r,
     rc_s, rc_r, rx_s, rx_r, ry_s, ry_r, rz_s, rz_r,
 ):
@@ -375,8 +375,6 @@
         return carry
 
     lax.fori_loop(0, NX, hidden_part, 0)
-    out = pltpu.make_async_copy(gh, gh_hbm, out_sem)
-    out.start()
 
     take_x(CH - 1)
     lax.fori_loop(0, CH, lambda j, carry: (take_y(j), carry)[1], 0)
@@ -426,7 +424,6 @@
     pltpu.make_async_copy(x_recv, x_recv, rx_s).wait()
     pltpu.make_async_copy(y_recv, y_recv, ry_s).wait()
 
-    out.wait()
     pltpu.make_async_copy(f_recv, f_recv, rz_r).wait()
     total = f_recv[0].astype(F32)
     for k in range(1, 8):
@@ -458,7 +455,7 @@
         ((CH, NX, NY, 32, 128), BF16), ((CH, NX, NY, 32, 128), BF16),
         ((CH, NX, NY, 32, 128), BF16), ((CH, NX - 1, NY, 32, 128), BF16),
         ((CH, NY, 32, 128), BF16), ((CH, NY - 1, 32, 128), BF16),
-        ((CH, 32, 128), BF16), ((8, 16, 128), BF16), ((8, 16, 128), BF16), ((TOK, 2048), BF16),
+        ((CH, 32, 128), BF16), ((8, 16, 128), BF16), ((8, 16, 128), BF16),
     ]
     return pl.pallas_call(
         functools.partial(kernel, scale),
@@ -467,10 +464,10 @@
             jax.ShapeDtypeStruct((4, 512), F32),
         ),
         in_specs=[hbm] * 5,
-        out_specs=(hbm, vmem),
+        out_specs=(vmem, vmem),
         scratch_shapes=[pltpu.VMEM(shape, kind) for shape, kind in scratch]
         + [
-            dma((5,)), dma,
+            dma((5,)),
             dma, dma, dma, dma((LAST, NY - 1)), dma, dma((LAST,)), dma, dma((NX - 1,)), dma, dma, dma, dma((CH,)),
             dma, dma((CH,)), dma, dma((CH, NY)), dma, dma((CH,)), dma, dma,
         ],

time: 58.7 us -> 58.7 us (level)
  no operation moved by 1% of the time
where the time goes in v6:
time: 58.7 us; the launch traced here: 58.6 us
  Pallas kernels  56.4 us (96%)
  local copies, waits for them, and re-layouts  1.57 us (3%)
  between operations  0.64 us (1%)
    pallas_call x1, Pallas kernels, on_device(): pl.pallas_call(functools.partial(kernel, scale), out_shape=(jax.ShapeDtyp...  56.4 us
    unnamed x2, local copies, waits for them, and re-layouts  1.57 us

profile of v6, /device:TPU:1, one launch (start us, length us, event | category | flops | bytes accessed | tf_op | source)
XLA Modules:
  0.0 58.6 jit_solution(11577279950590510903)
XLA Ops:
  0.6 56.4 %shard_map.68 = (bf16[256,2048]{1,0:T(8,128)(2,1)S(1)}, f32[4,512]{1,0:T(4,128)S(1)}) custom-call(bf16[256,2048]{1,0:T(8,128)(2,1)} %hid_hbm.1, bf16[256,1024]{1,0:T(8,128)(2,1)} %que_hbm.1, bf16[256,1024]{1,0:T(8,128)(2,1)} %cot_hbm.1, s32[1,256]{1,0:T(1,128)} %seg_hbm.1, bf16[4,512]{1,0:T(4,128)(2,1)} %kvw_hbm.1), custom_call_target="tpu_custom_call" | custom-call | tf_op jit(solution)/shard_map/pallas_call | solution.py:460
  57.0 1.0 %copy.9 = bf16[256,2048]{1,0:T(8,128)(2,1)} copy(bf16[256,2048]{1,0:T(8,128)(2,1)S(1)} %get-tuple-element.4) | data formatting | bytes 2097152
  58.0 0.6 %copy.10 = f32[4,512]{1,0:T(4,128)} copy(f32[4,512]{1,0:T(4,128)S(1)} %get-tuple-element.5) | data formatting | bytes 16384
